TPU v7x, 128 devices: a whole 4x4x4 slice. The times are simulated.
128 devices in a mesh: gx: 8 (over x, core), gy: 16 (over y, z).
Axes of the slice: x: 4, y: 4, z: 4, core: 2. Of those that a mesh axis runs over, the one named last changes fastest.
Arguments:
- pressure_source: float32 [192, 384, 384], P('gx', 'gy'), may hold values from -6 to 6
- building_heights: int32 [32, 64], replicated, may hold values from 0 to 63
Outputs:
- correction: float32 [192, 384, 384], P('gx', 'gy')
- coarse_solution: float32 [64, 128, 128], P('gx', 'gy')
Inputs may be any that keep to these rules, and one draw needn't show every extreme that they name: `building_heights`: the height of the building in each element column, in elements, so that the top layer of every column is fluid.
All inputs are finite; a program needn't handle non-finite values.
Results may differ from a plain program's by a relative error of at most 0.0003.
Values sent between devices are 32-bit elements; how exact they have to be, the bound alone decides.
No kernel may reach another device: no remote copies, remote signals or barrier semaphores. Data moves between devices by JAX's collectives and lax.ppermute only.
A program may use at most 128 MiB of HBM per device.

v0:
```python
import jax
import jax.numpy as jnp
import numpy as np
from jax import lax
from jax.sharding import PartitionSpec as P

CG_ITERS = 10
HIGHEST = lax.Precision.HIGHEST


def with_halo(cells, sides, width):
    for axis, dim in sides:
        count = lax.axis_size(axis)
        ends = count - 1
        head = lax.slice_in_dim(cells, 0, width, axis=dim)
        tail = lax.slice_in_dim(cells, cells.shape[dim] - width, cells.shape[dim], axis=dim)
        cells = jnp.concatenate(
            [
                lax.ppermute(tail, axis, [(i, (i + 1) % count) for i in range(ends)]),
                cells,
                lax.ppermute(head, axis, [((i + 1) % count, i) for i in range(ends)]),
            ],
            axis=dim,
        )
    return cells


def gll_nodes(node_count):
    if node_count == 6:
        outer_point = 0.7650553239294647
        inner_point = 0.2852315164806451
        points = [-1.0, -outer_point, -inner_point, inner_point, outer_point, 1.0]
        weights = [
            1.0 / 15.0,
            0.378474956297847,
            0.5548583770354863,
            0.5548583770354863,
            0.378474956297847,
            1.0 / 15.0,
        ]
    elif node_count == 4:
        inner_point = 0.4472135954999579
        points = [-1.0, -inner_point, inner_point, 1.0]
        weights = [1.0 / 6.0, 5.0 / 6.0, 5.0 / 6.0, 1.0 / 6.0]
    else:
        points = [-1.0, 1.0]
        weights = [1.0, 1.0]
    return (np.array(points), np.array(weights))


def diagonal_of(matrix):
    return np.array([matrix[index_id, index_id] for index_id in range(matrix.shape[0])])


def lagrange_tables(node_count):
    points, weights = gll_nodes(node_count)
    others = [
        [points[col_id] - points[other] for other in range(node_count) if other != col_id]
        for col_id in range(node_count)
    ]
    bary_weights = np.array([1.0 / np.prod(entries) for entries in others])
    derivative = np.zeros((node_count, node_count))
    for row_id in range(node_count):
        for col_id in range(node_count):
            if row_id != col_id:
                derivative[row_id, col_id] = (
                    bary_weights[col_id] / bary_weights[row_id] / (points[row_id] - points[col_id])
                )
        derivative[row_id, row_id] = -np.sum(derivative[row_id])
    stiffness = derivative.T @ (weights[:, None] * derivative)
    return (stiffness, weights)


def interpolation(coarse_count, fine_count):
    coarse_points = gll_nodes(coarse_count)[0]
    fine_points = gll_nodes(fine_count)[0]
    matrix = np.ones((fine_count, coarse_count))
    for row_id in range(fine_count):
        for col_id in range(coarse_count):
            for other in range(coarse_count):
                if other != col_id:
                    matrix[row_id, col_id] *= (fine_points[row_id] - coarse_points[other]) / (
                        coarse_points[col_id] - coarse_points[other]
                    )
    return matrix


def chebyshev_bounds(node_count):
    stiffness, weights = lagrange_tables(node_count)
    row_abs = np.abs(stiffness).sum(axis=1)
    diag_vals = diagonal_of(stiffness)
    wide_one = weights[:, None, None]
    wide_two = weights[None, :, None]
    wide_three = weights[None, None, :]
    numerator = (
        row_abs[:, None, None] * wide_two * wide_three
        + wide_one * row_abs[None, :, None] * wide_three
        + wide_one * wide_two * row_abs[None, None, :]
    )
    denominator = (
        diag_vals[:, None, None] * wide_two * wide_three
        + wide_one * diag_vals[None, :, None] * wide_three
        + wide_one * wide_two * diag_vals[None, None, :]
    )
    top_bound = float(np.max(numerator / denominator))
    return (top_bound, 0.1 * top_bound)


def tiled(vector, length, position):
    repeated = jnp.asarray(np.tile(vector, length // vector.shape[0]), jnp.float32)
    return repeated.reshape(tuple((length if axis_id == position else 1 for axis_id in range(3))))


def along_first(values, matrix):
    out_count, in_count = matrix.shape
    blocks = values.shape[0] // in_count
    shaped = values.reshape(blocks, in_count, values.shape[1] * values.shape[2])
    result = jnp.einsum("ip,xpr->xir", jnp.asarray(matrix, jnp.float32), shaped, precision=HIGHEST)
    return result.reshape(blocks * out_count, values.shape[1], values.shape[2])


def along_second(values, matrix):
    out_count, in_count = matrix.shape
    blocks = values.shape[1] // in_count
    shaped = values.reshape(values.shape[0], blocks, in_count, values.shape[2])
    result = jnp.einsum(
        "jq,xyqc->xyjc", jnp.asarray(matrix, jnp.float32), shaped, precision=HIGHEST
    )
    return result.reshape(values.shape[0], blocks * out_count, values.shape[2])


def along_third(values, matrix):
    out_count, in_count = matrix.shape
    blocks = values.shape[2] // in_count
    block_matrix = jnp.asarray(np.kron(np.eye(blocks), matrix.T), jnp.float32)
    result = jnp.dot(values.reshape(-1, values.shape[2]), block_matrix, precision=HIGHEST)
    return result.reshape(values.shape[0], values.shape[1], blocks * out_count)


def pass_first(padded, node_count):
    position = np.arange(padded.shape[0] - 2) % node_count
    at_start = jnp.asarray(position == 0, jnp.float32)[:, None, None]
    at_end = jnp.asarray(position == node_count - 1, jnp.float32)[:, None, None]
    return padded[1:-1] + at_start * padded[:-2] + at_end * padded[2:]


def pass_second(padded, node_count):
    position = np.arange(padded.shape[1] - 2) % node_count
    at_start = jnp.asarray(position == 0, jnp.float32)[None, :, None]
    at_end = jnp.asarray(position == node_count - 1, jnp.float32)[None, :, None]
    return padded[:, 1:-1] + at_start * padded[:, :-2] + at_end * padded[:, 2:]


def pass_third(values, node_count):
    position = np.arange(values.shape[2]) % node_count
    at_start = jnp.asarray(position == 0, jnp.float32)[None, None, :]
    at_end = jnp.asarray(position == node_count - 1, jnp.float32)[None, None, :]
    earlier = jnp.pad(values[:, :, :-1], ((0, 0), (0, 0), (1, 0)))
    following = jnp.pad(values[:, :, 1:], ((0, 0), (0, 0), (0, 1)))
    return values + at_start * earlier + at_end * following


def rim_joint(values):
    return with_halo(values, (("gx", 0), ("gy", 1)), 1)


def assemble(values, node_count):
    summed = pass_third(values, node_count)
    padded = rim_joint(summed)
    return pass_second(pass_first(padded, node_count), node_count)


def spread_counts(elem_pad, node_count):
    position = np.arange(node_count)
    at_start = jnp.asarray(position == 0, jnp.float32)
    at_end = jnp.asarray(position == node_count - 1, jnp.float32)
    step_one = (
        elem_pad[1:-1][:, None]
        + at_start[None, :, None, None] * elem_pad[:-2][:, None]
        + at_end[None, :, None, None] * elem_pad[2:][:, None]
    )
    step_one = step_one.reshape(-1, elem_pad.shape[1], elem_pad.shape[2])
    step_two = (
        step_one[:, 1:-1][:, :, None]
        + at_start[None, None, :, None] * step_one[:, :-2][:, :, None]
        + at_end[None, None, :, None] * step_one[:, 2:][:, :, None]
    )
    step_two = step_two.reshape(step_one.shape[0], -1, elem_pad.shape[2])
    step_three = (
        step_two[:, :, 1:-1][:, :, :, None]
        + at_start * step_two[:, :, :-2][:, :, :, None]
        + at_end * step_two[:, :, 2:][:, :, :, None]
    )
    return step_three.reshape(step_two.shape[0], step_two.shape[1], -1)


def level_data(fluid_pad, exist_pad, node_count):
    fluid_count = spread_counts(fluid_pad, node_count)
    exist_count = spread_counts(exist_pad, node_count)
    ground = jnp.asarray(np.arange(fluid_count.shape[2]) > 0, jnp.float32)[None, None, :]
    node_mask = (
        (fluid_count == exist_count).astype(jnp.float32)
        * (fluid_count > 0.5).astype(jnp.float32)
        * ground
    )
    node_weight = 1.0 / exist_count
    fluid_cells = fluid_pad[1:-1, 1:-1, 1:-1]
    fluid_node = jnp.repeat(
        jnp.repeat(jnp.repeat(fluid_cells, node_count, axis=0), node_count, axis=1),
        node_count,
        axis=2,
    )
    stiffness, weights = lagrange_tables(node_count)
    stiff_diag = diagonal_of(stiffness)
    dims_now = fluid_count.shape
    local_diag = (
        tiled(stiff_diag, dims_now[0], 0)
        * tiled(weights, dims_now[1], 1)
        * tiled(weights, dims_now[2], 2)
    )
    local_diag = local_diag + tiled(weights, dims_now[0], 0) * tiled(
        stiff_diag, dims_now[1], 1
    ) * tiled(weights, dims_now[2], 2)
    local_diag = local_diag + tiled(weights, dims_now[0], 0) * tiled(
        weights, dims_now[1], 1
    ) * tiled(stiff_diag, dims_now[2], 2)
    inverse_diag = node_mask / (fluid_count * local_diag + 1.0 - node_mask)
    return (node_count, fluid_node, node_mask, node_weight, inverse_diag)


def element_action(values, level_info):
    node_count, fluid_node = (level_info[0], level_info[1])
    stiffness, weights = lagrange_tables(node_count)
    mass_first = tiled(weights, values.shape[0], 0)
    mass_second = tiled(weights, values.shape[1], 1)
    mass_third = tiled(weights, values.shape[2], 2)
    summed_terms = mass_second * mass_third * along_first(values, stiffness)
    summed_terms = summed_terms + mass_first * mass_third * along_second(values, stiffness)
    summed_terms = summed_terms + mass_first * mass_second * along_third(values, stiffness)
    return fluid_node * summed_terms


def apply_operator(values, level_info, assembler):
    return level_info[2] * assembler(element_action(values, level_info), level_info[0])


def smooth(target, start, level_info, bounds, assembler, from_zero):
    top_bound, low_bound = bounds
    center = 0.5 * (top_bound + low_bound)
    half_width = 0.5 * (top_bound - low_bound)
    inverse_diag = level_info[4]
    if from_zero:
        residual_now = target
        update = inverse_diag * residual_now / center
        solution = update
    else:
        residual_now = target - apply_operator(start, level_info, assembler)
        update = inverse_diag * residual_now / center
        solution = start + update
    residual_now = residual_now - apply_operator(update, level_info, assembler)
    rho_first = half_width / center
    rho_next = 1.0 / (2.0 * center / half_width - rho_first)
    update = (
        rho_next * rho_first * update + 2.0 * rho_next / half_width * inverse_diag * residual_now
    )
    return solution + update


def restrict(values, coarse_count, fine_count):
    matrix = interpolation(coarse_count, fine_count).T
    return along_third(along_second(along_first(values, matrix), matrix), matrix)


def prolong(values, coarse_count, fine_count):
    matrix = interpolation(coarse_count, fine_count)
    return along_third(along_second(along_first(values, matrix), matrix), matrix)


def conjugate_gradients(target, level_info, assembler, reduce_sum):
    node_weight = level_info[3]
    norm_start = reduce_sum(jnp.sum(node_weight * target * target))

    def iterate(index, cg_state):
        solution, residual_now, direction, norm_now = cg_state
        applied = apply_operator(direction, level_info, assembler)
        step_len = norm_now / reduce_sum(jnp.sum(node_weight * direction * applied))
        solution = solution + step_len * direction
        residual_now = residual_now - step_len * applied
        norm_next = reduce_sum(jnp.sum(node_weight * residual_now * residual_now))
        direction = residual_now + norm_next / norm_now * direction
        return (solution, residual_now, direction, norm_next)

    final_state = lax.fori_loop(
        0, CG_ITERS, iterate, (jnp.zeros_like(target), target, target, norm_start)
    )
    return final_state[0]


def sum_spread(partial_sum):
    return lax.psum(partial_sum, ("gx", "gy"))


def coarse_spread(target, level_info):
    return conjugate_gradients(target, level_info, assemble, sum_spread)


def per_device(pressure_source, building_heights):
    side_first = pressure_source.shape[0] // 6
    side_second = pressure_source.shape[1] // 6
    column = pressure_source.shape[2] // 6
    start_first = lax.axis_index("gx") * side_first
    start_second = lax.axis_index("gy") * side_second
    heights_pad = jnp.pad(building_heights, 1, constant_values=column)
    local_heights = lax.dynamic_slice(
        heights_pad, (start_first, start_second), (side_first + 2, side_second + 2)
    )
    exist_cols = lax.dynamic_slice(
        jnp.pad(jnp.ones(building_heights.shape, jnp.float32), 1),
        (start_first, start_second),
        (side_first + 2, side_second + 2),
    )
    layers = jnp.arange(-1, column + 1, dtype=jnp.int32)
    inside = ((layers >= 0) & (layers < column)).astype(jnp.float32)[None, None, :]
    fluid_pad = (layers[None, None, :] >= local_heights[:, :, None]).astype(jnp.float32) * inside
    exist_pad = exist_cols[:, :, None] * inside
    fine_level = level_data(fluid_pad, exist_pad, 6)
    middle_level = level_data(fluid_pad, exist_pad, 4)
    coarse_level = level_data(fluid_pad, exist_pad, 2)
    fine_bounds = chebyshev_bounds(6)
    middle_bounds = chebyshev_bounds(4)
    target_fine = fine_level[2] * assemble(pressure_source, 6)
    fine_sol = smooth(target_fine, None, fine_level, fine_bounds, assemble, True)
    fine_res = target_fine - apply_operator(fine_sol, fine_level, assemble)
    target_middle = middle_level[2] * assemble(restrict(fine_level[3] * fine_res, 4, 6), 4)
    middle_sol = smooth(target_middle, None, middle_level, middle_bounds, assemble, True)
    middle_res = target_middle - apply_operator(middle_sol, middle_level, assemble)
    target_coarse = coarse_level[2] * assemble(restrict(middle_level[3] * middle_res, 2, 4), 2)
    coarse_sol = coarse_spread(target_coarse, coarse_level)
    middle_sol = middle_sol + middle_level[2] * prolong(coarse_sol, 2, 4)
    middle_sol = smooth(target_middle, middle_sol, middle_level, middle_bounds, assemble, False)
    fine_sol = fine_sol + fine_level[2] * prolong(middle_sol, 4, 6)
    fine_sol = smooth(target_fine, fine_sol, fine_level, fine_bounds, assemble, False)
    return (fine_sol, coarse_sol)


def solution(mesh):
    in_specs = (P("gx", "gy", None), P())
    out_specs = (P("gx", "gy", None), P("gx", "gy", None))
    return jax.shard_map(
        per_device, mesh=mesh, in_specs=in_specs, out_specs=out_specs, check_vma=False
    )
```

profile of v0, /device:TPU:105, one launch (start us, length us, event | category | flops | bytes accessed | tf_op | source)
XLA Modules:
  0.0 2164.7 jit_solution(11092381032411942674)
XLA Ops:
  30.0 4.7 copy.273
  45.0 4.7 copy.281
  59.9 4.7 copy.284
  275.1 5.7 collective-permute-start.26
  328.0 63.3 %psum.27 = f32[]{:T(128)} all-reduce(f32[]{:T(128)} %get-tuple-element.560), channel_id=1, replica_groups=mesh['gx'=8,'gy'=16] {'gx','gy'}, use_global_device_ids=true, to_apply=%region_1.2 | all-reduce | flops 1 | bytes 8 | tf_op jit(solution)/shard_map/psum | solution.py:300
  391.3 1636.0 %while.23 = (s32[]{:T(128)}, f32[8,8,128]{2,1,0:T(8,128)}, f32[8,8,128]{2,1,0:T(8,128)}, f32[8,8,128]{2,1,0:T(8,128)S(1)}, f32[]{:T(128)}, /*index=5*/f32[8,8,64...) while((s32[]{:T(128)}, f32[8,8,128]{2,1,0:T(8,128)}, ...), condition=%wide.region_7.8_spmd.clone.clone.clone.clone.clone, body=%wide.region_2.7_spmd.sunk.clone.clone.clone.clone.clone.sunk | while | flops 13401093 | bytes 2653795 | solution.py:293
  405.7 5.5 collective-permute-start.3
  424.1 63.5 %psum.42 = f32[]{:T(128)} all-reduce(f32[]{:T(128)} %get-tuple-element.823), channel_id=1, replica_groups=mesh['gx'=8,'gy'=16] {'gx','gy'}, use_global_device_ids=true, to_apply=%region_4.4 | all-reduce | flops 1 | bytes 8 | tf_op jit(solution)/shard_map/while/body/eval_jaxpr/psum | solution.py:300
  490.4 62.5 %psum.43 = f32[]{:T(128)} all-reduce(f32[]{:T(128)} %get-tuple-element.825), channel_id=1, replica_groups=mesh['gx'=8,'gy'=16] {'gx','gy'}, use_global_device_ids=true, to_apply=%region_6.6 | all-reduce | flops 1 | bytes 8 | tf_op jit(solution)/shard_map/while/body/eval_jaxpr/psum | solution.py:300
  587.4 63.8 %psum.42 = f32[]{:T(128)} all-reduce(f32[]{:T(128)} %get-tuple-element.823), channel_id=1, replica_groups=mesh['gx'=8,'gy'=16] {'gx','gy'}, use_global_device_ids=true, to_apply=%region_4.4 | all-reduce | flops 1 | bytes 8 | tf_op jit(solution)/shard_map/while/body/eval_jaxpr/psum | solution.py:300
  653.9 62.5 %psum.43 = f32[]{:T(128)} all-reduce(f32[]{:T(128)} %get-tuple-element.825), channel_id=1, replica_groups=mesh['gx'=8,'gy'=16] {'gx','gy'}, use_global_device_ids=true, to_apply=%region_6.6 | all-reduce | flops 1 | bytes 8 | tf_op jit(solution)/shard_map/while/body/eval_jaxpr/psum | solution.py:300
  733.6 4.7 collective-permute-start.3
  751.2 63.5 %psum.42 = f32[]{:T(128)} all-reduce(f32[]{:T(128)} %get-tuple-element.823), channel_id=1, replica_groups=mesh['gx'=8,'gy'=16] {'gx','gy'}, use_global_device_ids=true, to_apply=%region_4.4 | all-reduce | flops 1 | bytes 8 | tf_op jit(solution)/shard_map/while/body/eval_jaxpr/psum | solution.py:300
  817.5 62.5 %psum.43 = f32[]{:T(128)} all-reduce(f32[]{:T(128)} %get-tuple-element.825), channel_id=1, replica_groups=mesh['gx'=8,'gy'=16] {'gx','gy'}, use_global_device_ids=true, to_apply=%region_6.6 | all-reduce | flops 1 | bytes 8 | tf_op jit(solution)/shard_map/while/body/eval_jaxpr/psum | solution.py:300
  914.8 63.6 %psum.42 = f32[]{:T(128)} all-reduce(f32[]{:T(128)} %get-tuple-element.823), channel_id=1, replica_groups=mesh['gx'=8,'gy'=16] {'gx','gy'}, use_global_device_ids=true, to_apply=%region_4.4 | all-reduce | flops 1 | bytes 8 | tf_op jit(solution)/shard_map/while/body/eval_jaxpr/psum | solution.py:300
  981.1 62.5 %psum.43 = f32[]{:T(128)} all-reduce(f32[]{:T(128)} %get-tuple-element.825), channel_id=1, replica_groups=mesh['gx'=8,'gy'=16] {'gx','gy'}, use_global_device_ids=true, to_apply=%region_6.6 | all-reduce | flops 1 | bytes 8 | tf_op jit(solution)/shard_map/while/body/eval_jaxpr/psum | solution.py:300
  1060.8 4.7 collective-permute-start.3
  1078.4 63.6 %psum.42 = f32[]{:T(128)} all-reduce(f32[]{:T(128)} %get-tuple-element.823), channel_id=1, replica_groups=mesh['gx'=8,'gy'=16] {'gx','gy'}, use_global_device_ids=true, to_apply=%region_4.4 | all-reduce | flops 1 | bytes 8 | tf_op jit(solution)/shard_map/while/body/eval_jaxpr/psum | solution.py:300
  1144.7 62.5 %psum.43 = f32[]{:T(128)} all-reduce(f32[]{:T(128)} %get-tuple-element.825), channel_id=1, replica_groups=mesh['gx'=8,'gy'=16] {'gx','gy'}, use_global_device_ids=true, to_apply=%region_6.6 | all-reduce | flops 1 | bytes 8 | tf_op jit(solution)/shard_map/while/body/eval_jaxpr/psum | solution.py:300
  1224.3 4.7 collective-permute-start.3
  1242.0 63.6 %psum.42 = f32[]{:T(128)} all-reduce(f32[]{:T(128)} %get-tuple-element.823), channel_id=1, replica_groups=mesh['gx'=8,'gy'=16] {'gx','gy'}, use_global_device_ids=true, to_apply=%region_4.4 | all-reduce | flops 1 | bytes 8 | tf_op jit(solution)/shard_map/while/body/eval_jaxpr/psum | solution.py:300
  1308.3 62.5 %psum.43 = f32[]{:T(128)} all-reduce(f32[]{:T(128)} %get-tuple-element.825), channel_id=1, replica_groups=mesh['gx'=8,'gy'=16] {'gx','gy'}, use_global_device_ids=true, to_apply=%region_6.6 | all-reduce | flops 1 | bytes 8 | tf_op jit(solution)/shard_map/while/body/eval_jaxpr/psum | solution.py:300
  1405.6 63.6 %psum.42 = f32[]{:T(128)} all-reduce(f32[]{:T(128)} %get-tuple-element.823), channel_id=1, replica_groups=mesh['gx'=8,'gy'=16] {'gx','gy'}, use_global_device_ids=true, to_apply=%region_4.4 | all-reduce | flops 1 | bytes 8 | tf_op jit(solution)/shard_map/while/body/eval_jaxpr/psum | solution.py:300
  1471.8 62.5 %psum.43 = f32[]{:T(128)} all-reduce(f32[]{:T(128)} %get-tuple-element.825), channel_id=1, replica_groups=mesh['gx'=8,'gy'=16] {'gx','gy'}, use_global_device_ids=true, to_apply=%region_6.6 | all-reduce | flops 1 | bytes 8 | tf_op jit(solution)/shard_map/while/body/eval_jaxpr/psum | solution.py:300
  1569.2 63.6 %psum.42 = f32[]{:T(128)} all-reduce(f32[]{:T(128)} %get-tuple-element.823), channel_id=1, replica_groups=mesh['gx'=8,'gy'=16] {'gx','gy'}, use_global_device_ids=true, to_apply=%region_4.4 | all-reduce | flops 1 | bytes 8 | tf_op jit(solution)/shard_map/while/body/eval_jaxpr/psum | solution.py:300
  1635.4 62.5 %psum.43 = f32[]{:T(128)} all-reduce(f32[]{:T(128)} %get-tuple-element.825), channel_id=1, replica_groups=mesh['gx'=8,'gy'=16] {'gx','gy'}, use_global_device_ids=true, to_apply=%region_6.6 | all-reduce | flops 1 | bytes 8 | tf_op jit(solution)/shard_map/while/body/eval_jaxpr/psum | solution.py:300
  1732.7 63.6 %psum.42 = f32[]{:T(128)} all-reduce(f32[]{:T(128)} %get-tuple-element.823), channel_id=1, replica_groups=mesh['gx'=8,'gy'=16] {'gx','gy'}, use_global_device_ids=true, to_apply=%region_4.4 | all-reduce | flops 1 | bytes 8 | tf_op jit(solution)/shard_map/while/body/eval_jaxpr/psum | solution.py:300
  1799.0 62.5 %psum.43 = f32[]{:T(128)} all-reduce(f32[]{:T(128)} %get-tuple-element.825), channel_id=1, replica_groups=mesh['gx'=8,'gy'=16] {'gx','gy'}, use_global_device_ids=true, to_apply=%region_6.6 | all-reduce | flops 1 | bytes 8 | tf_op jit(solution)/shard_map/while/body/eval_jaxpr/psum | solution.py:300
  1878.7 4.7 collective-permute-start.3
  1896.3 63.6 %psum.42 = f32[]{:T(128)} all-reduce(f32[]{:T(128)} %get-tuple-element.823), channel_id=1, replica_groups=mesh['gx'=8,'gy'=16] {'gx','gy'}, use_global_device_ids=true, to_apply=%region_4.4 | all-reduce | flops 1 | bytes 8 | tf_op jit(solution)/shard_map/while/body/eval_jaxpr/psum | solution.py:300
  1962.6 62.5 %psum.43 = f32[]{:T(128)} all-reduce(f32[]{:T(128)} %get-tuple-element.825), channel_id=1, replica_groups=mesh['gx'=8,'gy'=16] {'gx','gy'}, use_global_device_ids=true, to_apply=%region_6.6 | all-reduce | flops 1 | bytes 8 | tf_op jit(solution)/shard_map/while/body/eval_jaxpr/psum | solution.py:300
  2056.4 4.7 collective-permute-done.35
  (1159 shorter events, 764.8 us)
Async XLA Ops:
  2.9 9.5 collective-permute-start.4
  13.1 59.8 %collective-permute-start.6 = (f32[26,1,384]{2,1,0:T(1,128)}, f32[26,1,384]{2,1,0:T(1,128)}, u32[]{:S(2)}, u32[]{:S(2)}) collective-permute-start(f32[26,1,384]{2,1,0:T(1,128)} %get-tuple-element.590), channel_id=1, source_target_pairs={{0,1},{1,2},{2,3},{3,4},{4,5},{5,6},{6,7},{7,8},{8,9},{9,10},{10,1... | collective-permute-start | bytes 119816 | tf_op jit(solution)/shard_map/ppermute | solution.py:19
  15.0 57.9 %collective-permute-start.7 = (f32[26,1,384]{2,1,0:T(1,128)}, f32[26,1,384]{2,1,0:T(1,128)}, u32[]{:S(2)}, u32[]{:S(2)}) collective-permute-start(f32[26,1,384]{2,1,0:T(1,128)} %get-tuple-element.591), channel_id=1, source_target_pairs={{1,0},{2,1},{3,2},{4,3},{5,4},{6,5},{7,6},{8,7},{9,8},{10,9},{11,1... | collective-permute-start | bytes 119816 | tf_op jit(solution)/shard_map/ppermute | solution.py:21
  102.8 7.0 collective-permute-start.10
  168.8 49.5 %collective-permute-start.18 = (f32[18,1,256]{2,1,0:T(1,128)}, f32[18,1,256]{2,1,0:T(1,128)}, u32[]{:S(2)}, u32[]{:S(2)}) collective-permute-start(f32[18,1,256]{2,1,0:T(1,128)} %get-tuple-element.620), channel_id=1, source_target_pairs={{0,1},{1,2},{2,3},{3,4},{4,5},{5,6},{6,7},{7,8},{8,9},{9,10},{10,1... | collective-permute-start | bytes 55304 | tf_op jit(solution)/shard_map/ppermute | solution.py:19
  170.7 47.6 %collective-permute-start.19 = (f32[18,1,256]{2,1,0:T(1,128)}, f32[18,1,256]{2,1,0:T(1,128)}, u32[]{:S(2)}, u32[]{:S(2)}) collective-permute-start(f32[18,1,256]{2,1,0:T(1,128)} %get-tuple-element.621), channel_id=1, source_target_pairs={{1,0},{2,1},{3,2},{4,3},{5,4},{6,5},{7,6},{8,7},{9,8},{10,9},{11,1... | collective-permute-start | bytes 55304 | tf_op jit(solution)/shard_map/ppermute | solution.py:21
  233.3 8.7 collective-permute-start.20
  242.8 11.7 collective-permute-start.22
  246.8 7.7 collective-permute-start.23
  275.1 8.4 collective-permute-start.26
  299.8 23.9 %collective-permute-start.30 = (f32[10,1,128]{2,1,0:T(1,128)}, f32[10,1,128]{2,1,0:T(1,128)}, u32[]{:S(2)}, u32[]{:S(2)}) collective-permute-start(f32[10,1,128]{2,1,0:T(1,128)} %get-tuple-element.666), channel_id=1, source_target_pairs={{0,1},{1,2},{2,3},{3,4},{4,5},{5,6},{6,7},{7,8},{8,9},{9,10},{10,1... | collective-permute-start | bytes 15368 | tf_op jit(solution)/shard_map/ppermute | solution.py:19
  301.7 22.0 %collective-permute-start.31 = (f32[10,1,128]{2,1,0:T(1,128)}, f32[10,1,128]{2,1,0:T(1,128)}, u32[]{:S(2)}, u32[]{:S(2)}) collective-permute-start(f32[10,1,128]{2,1,0:T(1,128)} %get-tuple-element.667), channel_id=1, source_target_pairs={{1,0},{2,1},{3,2},{4,3},{5,4},{6,5},{7,6},{8,7},{9,8},{10,9},{11,1... | collective-permute-start | bytes 15368 | tf_op jit(solution)/shard_map/ppermute | solution.py:21
  403.8 18.0 collective-permute-start.2
  405.7 16.1 collective-permute-start.3
  567.1 18.0 collective-permute-start.2
  570.0 15.1 collective-permute-start.3
  730.9 18.0 collective-permute-start.2
  733.6 15.3 collective-permute-start.3
  894.4 18.0 collective-permute-start.2
  897.2 15.3 collective-permute-start.3
  1058.0 18.0 collective-permute-start.2
  1060.8 15.3 collective-permute-start.3
  1221.6 18.0 collective-permute-start.2
  1224.3 15.3 collective-permute-start.3
  1385.2 18.0 collective-permute-start.2
  1387.9 15.3 collective-permute-start.3
  1548.8 18.0 collective-permute-start.2
  1551.5 15.3 collective-permute-start.3
  1712.4 18.0 collective-permute-start.2
  1715.1 15.3 collective-permute-start.3
  1876.0 18.0 collective-permute-start.2
  1878.7 15.3 collective-permute-start.3
  (257 other events, 1680.2 us)
where the time goes:
time: 2180 us; the launch traced here: 2160 us
  blocking collectives  1320 us (61%)
  local copies, waits for them, and re-layouts  303 us (14%)
  starting transfers between devices  256 us (12%)
  other arithmetic  103 us (5%)
  matrix products  92.5 us (4%)
  waiting for transfers between devices  59.1 us (3%)
  loops' own time  22.8 us (1%)
    psum x21, blocking collectives, sum_spread(): return lax.psum(partial_sum, ('gx', 'gy'))  1320 us
    ppermute x42, starting transfers between devices, with_halo(): lax.ppermute(tail, axis, [(i, (i + 1) % count) for i in range(ends)])  150 us
    ppermute x42, starting transfers between devices, with_halo(): lax.ppermute(head, axis, [((i + 1) % count, i) for i in range(ends)])  106 us
    mul x58, local copies, waits for them, and re-layouts, spread_counts(): at_end * step_two[:, :, 2:][:, :, :, None]  67 us
    add x52, local copies, waits for them, and re-layouts, spread_counts(): step_two[:, :, 1:-1][:, :, :, None]  64.9 us
    mul x58, local copies, waits for them, and re-layouts, spread_counts(): at_start * step_two[:, :, :-2][:, :, :, None]  54.8 us
    ppermute x42, waiting for transfers between devices, with_halo(): lax.ppermute(head, axis, [((i + 1) % count, i) for i in range(ends)])  51.8 us
  transfers between devices with their start and end apart: 84, of which 26 were waited for; matrix products, arithmetic and copies ran while one was open for 11% of the time, Pallas kernels for 0%

commit v1 on v0

--- a/solution.py
+++ b/solution.py
@@ -297,7 +297,7 @@
 
 
 def sum_spread(partial_sum):
-    return lax.psum(partial_sum, ("gx", "gy"))
+    return lax.psum(lax.psum(partial_sum, "gy"), "gx")
 
 
 def coarse_spread(target, level_info):

time: 2180 us -> 1870 us (0.86)
  blocking collectives: 1320 us -> 1010 us
    psum x21 -> x42, blocking collectives: 1320 us -> 1010 us  [sum_spread(): return lax.psum(lax.psum(partial_sum, 'gy'), 'gx')]
    ppermute x42, starting transfers between devices: 150 us -> 126 us  [with_halo(): lax.ppermute(tail, axis, [(i, (i + 1) % count) for i in range(ends)])]
  transfers between devices with their start and end apart: 84 -> 84, of which waited for: 26 -> 28; matrix products, arithmetic and copies ran while one was open for 11% -> 12% of each run, Pallas kernels for 0% -> 0%
where the time goes in v1:
time: 1870 us; the launch traced here: 1850 us
  blocking collectives  1010 us (54%)
  local copies, waits for them, and re-layouts  306 us (16%)
  starting transfers between devices  248 us (13%)
  other arithmetic  101 us (5%)
  matrix products  92.5 us (5%)
  waiting for transfers between devices  63.6 us (3%)
  loops' own time  22.2 us (1%)
    psum x42, blocking collectives, sum_spread(): return lax.psum(lax.psum(partial_sum, 'gy'), 'gx')  1010 us
    ppermute x42, starting transfers between devices, with_halo(): lax.ppermute(tail, axis, [(i, (i + 1) % count) for i in range(ends)])  126 us
    ppermute x42, starting transfers between devices, with_halo(): lax.ppermute(head, axis, [((i + 1) % count, i) for i in range(ends)])  122 us
    mul x58, local copies, waits for them, and re-layouts, spread_counts(): at_end * step_two[:, :, 2:][:, :, :, None]  69.8 us
    add x52, local copies, waits for them, and re-layouts, spread_counts(): step_two[:, :, 1:-1][:, :, :, None]  66.9 us
    mul x58, local copies, waits for them, and re-layouts, spread_counts(): at_start * step_two[:, :, :-2][:, :, :, None]  57.4 us
    ppermute x42, waiting for transfers between devices, with_halo(): lax.ppermute(head, axis, [((i + 1) % count, i) for i in range(ends)])  56.3 us
  transfers between devices with their start and end apart: 84, of which 28 were waited for; matrix products, arithmetic and copies ran while one was open for 12% of the time, Pallas kernels for 0%

profile of v1, /device:TPU:105, one launch (start us, length us, event | category | flops | bytes accessed | tf_op | source)
XLA Modules:
  0.0 1851.7 jit_solution(17920811781715666761)
XLA Ops:
  329.8 24.4 %psum.54 = f32[]{:T(128)} all-reduce(f32[]{:T(128)} %get-tuple-element.560), channel_id=1, replica_groups=mesh['gx'=8,'gy'=16] {'gy'}, use_global_device_ids=true, to_apply=%region_1.2 | all-reduce | flops 1 | bytes 8 | tf_op jit(solution)/shard_map/psum | solution.py:300
  373.6 1340.5 %while.23 = (s32[]{:T(128)}, f32[8,8,128]{2,1,0:T(8,128)}, f32[8,8,128]{2,1,0:T(8,128)}, f32[8,8,128]{2,1,0:T(8,128)S(1)}, f32[]{:T(128)}, /*index=5*/f32[8,8,64...) while((s32[]{:T(128)}, f32[8,8,128]{2,1,0:T(8,128)}, ...), condition=%wide.region_10.11_spmd.clone.clone.clone.clone.clone, body=%wide.region_3.10_spmd.sunk.clone.clone.clone.clone.clone.sunk | while | flops 13401095 | bytes 2653811 | solution.py:293
  406.0 24.4 %psum.84 = f32[]{:T(128)} all-reduce(f32[]{:T(128)} %get-tuple-element.823), channel_id=1, replica_groups=mesh['gx'=8,'gy'=16] {'gy'}, use_global_device_ids=true, to_apply=%region_5.5 | all-reduce | flops 1 | bytes 8 | tf_op jit(solution)/shard_map/while/body/eval_jaxpr/psum | solution.py:300
  452.4 28.1 %psum.86 = f32[]{:T(128)} all-reduce(f32[]{:T(128)} %get-tuple-element.825), channel_id=1, replica_groups=mesh['gx'=8,'gy'=16] {'gy'}, use_global_device_ids=true, to_apply=%region_8.8 | all-reduce | flops 1 | bytes 8 | tf_op jit(solution)/shard_map/while/body/eval_jaxpr/psum | solution.py:300
  534.3 28.8 %psum.84 = f32[]{:T(128)} all-reduce(f32[]{:T(128)} %get-tuple-element.823), channel_id=1, replica_groups=mesh['gx'=8,'gy'=16] {'gy'}, use_global_device_ids=true, to_apply=%region_5.5 | all-reduce | flops 1 | bytes 8 | tf_op jit(solution)/shard_map/while/body/eval_jaxpr/psum | solution.py:300
  563.1 19.7 %psum.85 = f32[]{:T(128)} all-reduce(f32[]{:T(128)} %psum.84), channel_id=1, replica_groups=mesh['gx'=8,'gy'=16] {'gx'}, use_global_device_ids=true, to_apply=%region_6.6 | all-reduce | flops 1 | bytes 8 | tf_op jit(solution)/shard_map/while/body/eval_jaxpr/psum | solution.py:300
  585.4 29.2 %psum.86 = f32[]{:T(128)} all-reduce(f32[]{:T(128)} %get-tuple-element.825), channel_id=1, replica_groups=mesh['gx'=8,'gy'=16] {'gy'}, use_global_device_ids=true, to_apply=%region_8.8 | all-reduce | flops 1 | bytes 8 | tf_op jit(solution)/shard_map/while/body/eval_jaxpr/psum | solution.py:300
  614.6 20.0 %psum.87 = f32[]{:T(128)} all-reduce(f32[]{:T(128)} %psum.86), channel_id=1, replica_groups=mesh['gx'=8,'gy'=16] {'gx'}, use_global_device_ids=true, to_apply=%region_9.9 | all-reduce | flops 1 | bytes 8 | tf_op jit(solution)/shard_map/while/body/eval_jaxpr/psum | solution.py:300
  668.9 28.8 %psum.84 = f32[]{:T(128)} all-reduce(f32[]{:T(128)} %get-tuple-element.823), channel_id=1, replica_groups=mesh['gx'=8,'gy'=16] {'gy'}, use_global_device_ids=true, to_apply=%region_5.5 | all-reduce | flops 1 | bytes 8 | tf_op jit(solution)/shard_map/while/body/eval_jaxpr/psum | solution.py:300
  720.1 29.2 %psum.86 = f32[]{:T(128)} all-reduce(f32[]{:T(128)} %get-tuple-element.825), channel_id=1, replica_groups=mesh['gx'=8,'gy'=16] {'gy'}, use_global_device_ids=true, to_apply=%region_8.8 | all-reduce | flops 1 | bytes 8 | tf_op jit(solution)/shard_map/while/body/eval_jaxpr/psum | solution.py:300
  749.3 20.0 %psum.87 = f32[]{:T(128)} all-reduce(f32[]{:T(128)} %psum.86), channel_id=1, replica_groups=mesh['gx'=8,'gy'=16] {'gx'}, use_global_device_ids=true, to_apply=%region_9.9 | all-reduce | flops 1 | bytes 8 | tf_op jit(solution)/shard_map/while/body/eval_jaxpr/psum | solution.py:300
  803.6 28.8 %psum.84 = f32[]{:T(128)} all-reduce(f32[]{:T(128)} %get-tuple-element.823), channel_id=1, replica_groups=mesh['gx'=8,'gy'=16] {'gy'}, use_global_device_ids=true, to_apply=%region_5.5 | all-reduce | flops 1 | bytes 8 | tf_op jit(solution)/shard_map/while/body/eval_jaxpr/psum | solution.py:300
  854.7 29.2 %psum.86 = f32[]{:T(128)} all-reduce(f32[]{:T(128)} %get-tuple-element.825), channel_id=1, replica_groups=mesh['gx'=8,'gy'=16] {'gy'}, use_global_device_ids=true, to_apply=%region_8.8 | all-reduce | flops 1 | bytes 8 | tf_op jit(solution)/shard_map/while/body/eval_jaxpr/psum | solution.py:300
  883.9 20.0 %psum.87 = f32[]{:T(128)} all-reduce(f32[]{:T(128)} %psum.86), channel_id=1, replica_groups=mesh['gx'=8,'gy'=16] {'gx'}, use_global_device_ids=true, to_apply=%region_9.9 | all-reduce | flops 1 | bytes 8 | tf_op jit(solution)/shard_map/while/body/eval_jaxpr/psum | solution.py:300
  938.2 28.8 %psum.84 = f32[]{:T(128)} all-reduce(f32[]{:T(128)} %get-tuple-element.823), channel_id=1, replica_groups=mesh['gx'=8,'gy'=16] {'gy'}, use_global_device_ids=true, to_apply=%region_5.5 | all-reduce | flops 1 | bytes 8 | tf_op jit(solution)/shard_map/while/body/eval_jaxpr/psum | solution.py:300
  989.4 29.2 %psum.86 = f32[]{:T(128)} all-reduce(f32[]{:T(128)} %get-tuple-element.825), channel_id=1, replica_groups=mesh['gx'=8,'gy'=16] {'gy'}, use_global_device_ids=true, to_apply=%region_8.8 | all-reduce | flops 1 | bytes 8 | tf_op jit(solution)/shard_map/while/body/eval_jaxpr/psum | solution.py:300
  1018.6 20.0 %psum.87 = f32[]{:T(128)} all-reduce(f32[]{:T(128)} %psum.86), channel_id=1, replica_groups=mesh['gx'=8,'gy'=16] {'gx'}, use_global_device_ids=true, to_apply=%region_9.9 | all-reduce | flops 1 | bytes 8 | tf_op jit(solution)/shard_map/while/body/eval_jaxpr/psum | solution.py:300
  1072.9 28.8 %psum.84 = f32[]{:T(128)} all-reduce(f32[]{:T(128)} %get-tuple-element.823), channel_id=1, replica_groups=mesh['gx'=8,'gy'=16] {'gy'}, use_global_device_ids=true, to_apply=%region_5.5 | all-reduce | flops 1 | bytes 8 | tf_op jit(solution)/shard_map/while/body/eval_jaxpr/psum | solution.py:300
  1124.1 29.2 %psum.86 = f32[]{:T(128)} all-reduce(f32[]{:T(128)} %get-tuple-element.825), channel_id=1, replica_groups=mesh['gx'=8,'gy'=16] {'gy'}, use_global_device_ids=true, to_apply=%region_8.8 | all-reduce | flops 1 | bytes 8 | tf_op jit(solution)/shard_map/while/body/eval_jaxpr/psum | solution.py:300
  1153.2 20.0 %psum.87 = f32[]{:T(128)} all-reduce(f32[]{:T(128)} %psum.86), channel_id=1, replica_groups=mesh['gx'=8,'gy'=16] {'gx'}, use_global_device_ids=true, to_apply=%region_9.9 | all-reduce | flops 1 | bytes 8 | tf_op jit(solution)/shard_map/while/body/eval_jaxpr/psum | solution.py:300
  1207.6 28.8 %psum.84 = f32[]{:T(128)} all-reduce(f32[]{:T(128)} %get-tuple-element.823), channel_id=1, replica_groups=mesh['gx'=8,'gy'=16] {'gy'}, use_global_device_ids=true, to_apply=%region_5.5 | all-reduce | flops 1 | bytes 8 | tf_op jit(solution)/shard_map/while/body/eval_jaxpr/psum | solution.py:300
  1258.7 29.2 %psum.86 = f32[]{:T(128)} all-reduce(f32[]{:T(128)} %get-tuple-element.825), channel_id=1, replica_groups=mesh['gx'=8,'gy'=16] {'gy'}, use_global_device_ids=true, to_apply=%region_8.8 | all-reduce | flops 1 | bytes 8 | tf_op jit(solution)/shard_map/while/body/eval_jaxpr/psum | solution.py:300
  1287.9 20.0 %psum.87 = f32[]{:T(128)} all-reduce(f32[]{:T(128)} %psum.86), channel_id=1, replica_groups=mesh['gx'=8,'gy'=16] {'gx'}, use_global_device_ids=true, to_apply=%region_9.9 | all-reduce | flops 1 | bytes 8 | tf_op jit(solution)/shard_map/while/body/eval_jaxpr/psum | solution.py:300
  1342.2 28.8 %psum.84 = f32[]{:T(128)} all-reduce(f32[]{:T(128)} %get-tuple-element.823), channel_id=1, replica_groups=mesh['gx'=8,'gy'=16] {'gy'}, use_global_device_ids=true, to_apply=%region_5.5 | all-reduce | flops 1 | bytes 8 | tf_op jit(solution)/shard_map/while/body/eval_jaxpr/psum | solution.py:300
  1393.4 29.2 %psum.86 = f32[]{:T(128)} all-reduce(f32[]{:T(128)} %get-tuple-element.825), channel_id=1, replica_groups=mesh['gx'=8,'gy'=16] {'gy'}, use_global_device_ids=true, to_apply=%region_8.8 | all-reduce | flops 1 | bytes 8 | tf_op jit(solution)/shard_map/while/body/eval_jaxpr/psum | solution.py:300
  1422.6 20.0 %psum.87 = f32[]{:T(128)} all-reduce(f32[]{:T(128)} %psum.86), channel_id=1, replica_groups=mesh['gx'=8,'gy'=16] {'gx'}, use_global_device_ids=true, to_apply=%region_9.9 | all-reduce | flops 1 | bytes 8 | tf_op jit(solution)/shard_map/while/body/eval_jaxpr/psum | solution.py:300
  1476.9 28.8 %psum.84 = f32[]{:T(128)} all-reduce(f32[]{:T(128)} %get-tuple-element.823), channel_id=1, replica_groups=mesh['gx'=8,'gy'=16] {'gy'}, use_global_device_ids=true, to_apply=%region_5.5 | all-reduce | flops 1 | bytes 8 | tf_op jit(solution)/shard_map/while/body/eval_jaxpr/psum | solution.py:300
  1528.0 29.2 %psum.86 = f32[]{:T(128)} all-reduce(f32[]{:T(128)} %get-tuple-element.825), channel_id=1, replica_groups=mesh['gx'=8,'gy'=16] {'gy'}, use_global_device_ids=true, to_apply=%region_8.8 | all-reduce | flops 1 | bytes 8 | tf_op jit(solution)/shard_map/while/body/eval_jaxpr/psum | solution.py:300
  1557.2 20.0 %psum.87 = f32[]{:T(128)} all-reduce(f32[]{:T(128)} %psum.86), channel_id=1, replica_groups=mesh['gx'=8,'gy'=16] {'gx'}, use_global_device_ids=true, to_apply=%region_9.9 | all-reduce | flops 1 | bytes 8 | tf_op jit(solution)/shard_map/while/body/eval_jaxpr/psum | solution.py:300
  1611.6 28.8 %psum.84 = f32[]{:T(128)} all-reduce(f32[]{:T(128)} %get-tuple-element.823), channel_id=1, replica_groups=mesh['gx'=8,'gy'=16] {'gy'}, use_global_device_ids=true, to_apply=%region_5.5 | all-reduce | flops 1 | bytes 8 | tf_op jit(solution)/shard_map/while/body/eval_jaxpr/psum | solution.py:300
  1662.7 29.2 %psum.86 = f32[]{:T(128)} all-reduce(f32[]{:T(128)} %get-tuple-element.825), channel_id=1, replica_groups=mesh['gx'=8,'gy'=16] {'gy'}, use_global_device_ids=true, to_apply=%region_8.8 | all-reduce | flops 1 | bytes 8 | tf_op jit(solution)/shard_map/while/body/eval_jaxpr/psum | solution.py:300
  1691.9 20.0 %psum.87 = f32[]{:T(128)} all-reduce(f32[]{:T(128)} %psum.86), channel_id=1, replica_groups=mesh['gx'=8,'gy'=16] {'gx'}, use_global_device_ids=true, to_apply=%region_9.9 | all-reduce | flops 1 | bytes 8 | tf_op jit(solution)/shard_map/while/body/eval_jaxpr/psum | solution.py:300
  (1230 shorter events, 1025.9 us)
Async XLA Ops:
  2.9 9.5 collective-permute-start.4
  13.1 59.8 %collective-permute-start.6 = (f32[26,1,384]{2,1,0:T(1,128)}, f32[26,1,384]{2,1,0:T(1,128)}, u32[]{:S(2)}, u32[]{:S(2)}) collective-permute-start(f32[26,1,384]{2,1,0:T(1,128)} %get-tuple-element.590), channel_id=1, source_target_pairs={{0,1},{1,2},{2,3},{3,4},{4,5},{5,6},{6,7},{7,8},{8,9},{9,10},{10,1... | collective-permute-start | bytes 119816 | tf_op jit(solution)/shard_map/ppermute | solution.py:19
  15.0 57.9 %collective-permute-start.7 = (f32[26,1,384]{2,1,0:T(1,128)}, f32[26,1,384]{2,1,0:T(1,128)}, u32[]{:S(2)}, u32[]{:S(2)}) collective-permute-start(f32[26,1,384]{2,1,0:T(1,128)} %get-tuple-element.591), channel_id=1, source_target_pairs={{1,0},{2,1},{3,2},{4,3},{5,4},{6,5},{7,6},{8,7},{9,8},{10,9},{11,1... | collective-permute-start | bytes 119816 | tf_op jit(solution)/shard_map/ppermute | solution.py:21
  102.8 7.0 collective-permute-start.10
  106.7 6.8 collective-permute-start.11
  140.3 6.8 collective-permute-start.15
  170.2 55.3 %collective-permute-start.18 = (f32[18,1,256]{2,1,0:T(1,128)S(1)}, f32[18,1,256]{2,1,0:T(1,128)S(1)}, u32[]{:S(2)}, u32[]{:S(2)}) collective-permute-start(f32[18,1,256]{2,1,0:T(1,128)S(1)} %get-tuple-element.620), channel_id=1, source_target_pairs={{0,1},{1,2},{2,3},{3,4},{4,5},{5,6},{6,7},{7,8},{8,9},{9,10},{10,1... | collective-permute-start | bytes 55304 | tf_op jit(solution)/shard_map/ppermute | solution.py:19
  172.2 54.0 %collective-permute-start.19 = (f32[18,1,256]{2,1,0:T(1,128)S(1)}, f32[18,1,256]{2,1,0:T(1,128)}, u32[]{:S(2)}, u32[]{:S(2)}) collective-permute-start(f32[18,1,256]{2,1,0:T(1,128)S(1)} %get-tuple-element.621), channel_id=1, source_target_pairs={{1,0},{2,1},{3,2},{4,3},{5,4},{6,5},{7,6},{8,7},{9,8},{10,9},{11,1... | collective-permute-start | bytes 55304 | tf_op jit(solution)/shard_map/ppermute | solution.py:21
  250.1 7.4 collective-permute-start.22
  301.7 24.5 %collective-permute-start.30 = (f32[10,1,128]{2,1,0:T(1,128)}, f32[10,1,128]{2,1,0:T(1,128)}, u32[]{:S(2)}, u32[]{:S(2)}) collective-permute-start(f32[10,1,128]{2,1,0:T(1,128)} %get-tuple-element.666), channel_id=1, source_target_pairs={{0,1},{1,2},{2,3},{3,4},{4,5},{5,6},{6,7},{7,8},{8,9},{9,10},{10,1... | collective-permute-start | bytes 15368 | tf_op jit(solution)/shard_map/ppermute | solution.py:19
  303.6 22.6 %collective-permute-start.31 = (f32[10,1,128]{2,1,0:T(1,128)}, f32[10,1,128]{2,1,0:T(1,128)}, u32[]{:S(2)}, u32[]{:S(2)}) collective-permute-start(f32[10,1,128]{2,1,0:T(1,128)} %get-tuple-element.667), channel_id=1, source_target_pairs={{1,0},{2,1},{3,2},{4,3},{5,4},{6,5},{7,6},{8,7},{9,8},{10,9},{11,1... | collective-permute-start | bytes 15368 | tf_op jit(solution)/shard_map/ppermute | solution.py:21
  385.5 18.2 collective-permute-start.2
  387.5 16.2 collective-permute-start.3
  514.0 18.0 collective-permute-start.2
  518.5 13.4 collective-permute-start.3
  648.6 18.0 collective-permute-start.2
  653.2 13.4 collective-permute-start.3
  783.3 18.0 collective-permute-start.2
  787.8 13.4 collective-permute-start.3
  918.0 18.0 collective-permute-start.2
  922.5 13.4 collective-permute-start.3
  1052.6 18.0 collective-permute-start.2
  1057.1 13.4 collective-permute-start.3
  1187.3 18.0 collective-permute-start.2
  1191.8 13.5 collective-permute-start.3
  1322.0 18.0 collective-permute-start.2
  1326.5 13.5 collective-permute-start.3
  1456.6 18.0 collective-permute-start.2
  1461.1 13.5 collective-permute-start.3
  1591.3 18.0 collective-permute-start.2
  1595.8 13.5 collective-permute-start.3
  1807.3 6.8 collective-permute-start.43
  (282 other events, 1864.5 us)
